TPU v7x, 128 devices: a whole 4x4x4 slice. The times are simulated.
128 devices in a mesh: ctx: 16 (over z_lo, x, core), wide: 8 (over z_hi, y).
Axes of the slice: x: 4, y: 4, z: 4 (z_hi: 2, z_lo: 2; z = z_hi * 2 + z_lo), core: 2. Of those that a mesh axis runs over, the one named last changes fastest.
Arguments:
- queries: bfloat16 [2048, 4, 4096], P('ctx', None, 'wide'), may hold values from -80 to 80
- new_entries: bfloat16 [2048, 4, 1024], P('ctx', None, 'wide'), may hold values from -8 to 8
- cached_entries: bfloat16 [8192, 4, 1024], P('ctx', None, 'wide'), may hold values from -12 to 12
- cache_lengths: int32 [4], replicated, may hold values from 1024 to 8192, as said below
- residual: bfloat16 [2048, 4, 2880], P(('ctx', 'wide')), may hold values from -6 to 6
- out_weight: bfloat16 [4096, 2880], P('wide', 'ctx'), may hold values from -0.09375 to 0.09375
- norm_gain: float32 [2880], replicated, may hold values from 0.1 to 1.9
- route_experts: int32 [2048, 4, 4], P(('ctx', 'wide')), may hold values from 0 to 127, all different within a row; in each aligned block of 64 rows (0 to 63, 64 to 127, ..., all dimensions but the last counted through in order) at most 4 rows name the same one
- route_weights: float32 [2048, 4, 4], P(('ctx', 'wide')), may hold values from 0.1 to 0.6
- inner_weight: bfloat16 [128, 2880, 2880], P(('ctx', 'wide')), may hold values from -0.109375 to 0.109375
- outer_weight: bfloat16 [128, 1440, 2880], P(('ctx', 'wide')), may hold values from -0.15625 to 0.15625
Outputs:
- layer_out: bfloat16 [2048, 4, 2880], P(('ctx', 'wide'))
Inputs may be any that keep to these rules, and one draw needn't show every extreme that they name: The cached positions of prompt p in use are 0 to cache_lengths[p] - 1, and the stretch follows them; some prompt uses all 8192 positions. `route_experts`: each token names 4 different experts; among the 64 tokens of one device (aligned blocks of rows in stretch then prompt order) no expert is named more than 4 times, and that many in some block.
All inputs are finite; a program needn't handle non-finite values.
Results may differ from a plain program's by a relative error of at most 0.018.
Values may be sent and summed in bfloat16 or wider, within the bound.
No kernel may reach another device: no remote copies, remote signals or barrier semaphores. Data moves between devices by JAX's collectives and lax.ppermute only.
A program may use at most 384 MiB of HBM per device.

v0:
```python
import jax
import jax.numpy as jnp
from jax import lax
from jax.sharding import PartitionSpec as P

HEAD_DIM = 64


NEGATIVE = -1e30


def absorb(carry, query_block, entries, allowed):
    best, total, accum = carry
    count = entries.shape[0]
    paired = entries.reshape(count, entries.shape[1], -1, 2, HEAD_DIM)
    keys = paired[:, :, :, 0]
    values = paired[:, :, :, 1]
    scores = (
        jnp.einsum("tpghd,jpgd->pghtj", query_block, keys, preferred_element_type=jnp.float32)
        * 0.125
    )
    masked = jnp.where(allowed, scores, NEGATIVE)
    fresh = jnp.maximum(best, jnp.max(masked, axis=-1))
    weights = jnp.where(allowed, jnp.exp(scores - fresh[..., None]), 0.0)
    decay = jnp.exp(best - fresh)
    total = total * decay + jnp.sum(weights, axis=-1)
    update = jnp.einsum(
        "pghtj,jpgd->pghtd",
        weights.astype(jnp.bfloat16),
        values,
        preferred_element_type=jnp.float32,
    )
    accum = accum * decay[..., None] + update
    return (fresh, total, accum)


def empty_carry(prompts, kv_local, group, rows):
    best = jnp.full((prompts, kv_local, group, rows), NEGATIVE, jnp.float32)
    total = jnp.zeros((prompts, kv_local, group, rows), jnp.float32)
    accum = jnp.zeros((prompts, kv_local, group, rows, HEAD_DIM), jnp.float32)
    return (best, total, accum)


def run_expert(batch, inner, outer):
    leading = batch.shape[:-1]
    rows = batch.reshape(-1, batch.shape[-1])
    lifted = jnp.dot(rows, inner, preferred_element_type=jnp.float32)
    half = lifted.shape[1] // 2
    gate = lifted[:, :half]
    upper = lifted[:, half:]
    active = ((upper + 1.0) * gate * jax.nn.sigmoid(1.702 * gate)).astype(jnp.bfloat16)
    result = jnp.dot(active, outer, preferred_element_type=jnp.float32).astype(jnp.bfloat16)
    return result.reshape(leading + (result.shape[-1],))


def shards(
    queries,
    new_entries,
    cached_entries,
    cache_lengths,
    residual,
    out_weight,
    norm_gain,
    route_experts,
    route_weights,
    inner_weight,
    outer_weight,
):
    local_rows, prompts, query_width = queries.shape
    kv_local = cached_entries.shape[2] // (2 * HEAD_DIM)
    group = query_width // (kv_local * HEAD_DIM)
    ctx_count = lax.axis_size("ctx")
    wide_count = lax.axis_size("wide")
    query_block = queries.reshape(local_rows, prompts, kv_local, group, HEAD_DIM)
    own_rows = lax.axis_index("ctx") * local_rows + jnp.arange(local_rows)
    start_carry = empty_carry(prompts, kv_local, group, local_rows)
    recent = lax.all_gather(new_entries, "ctx", axis=0, tiled=True)
    stretch_len = recent.shape[0]
    causal = (jnp.arange(stretch_len)[None, :] <= own_rows[:, None])[None, None, None]
    carry = absorb(start_carry, query_block, recent, causal)
    piece = lax.all_gather(cached_entries, "ctx", axis=0, tiled=True)
    positions = jnp.arange(piece.shape[0])
    allowed = (positions[None, :] < cache_lengths[:, None])[:, None, None, None, :]
    best, total, accum = absorb(carry, query_block, piece, allowed)
    attended = (
        (accum / total[..., None])
        .transpose(3, 0, 1, 2, 4)
        .reshape(local_rows, prompts, query_width)
        .astype(jnp.bfloat16)
    )
    full_weight = lax.all_gather(out_weight, "ctx", axis=1, tiled=True)
    count = lax.axis_size("wide") * (local_rows // wide_count)
    product = jnp.dot(
        attended.reshape(count * prompts, query_width),
        full_weight,
        preferred_element_type=jnp.float32,
    )
    projected = lax.psum_scatter(
        product.reshape(count, prompts, -1).astype(jnp.bfloat16),
        "wide",
        scatter_dimension=0,
        tiled=True,
    ).astype(jnp.float32)
    hidden = residual.astype(jnp.float32) + projected
    width = hidden.shape[-1]
    flat_hidden = hidden.reshape(-1, width)
    scale = lax.rsqrt(jnp.mean(flat_hidden * flat_hidden, axis=-1, keepdims=True) + 1e-05)
    normed = (flat_hidden * scale * norm_gain[None, :]).astype(jnp.bfloat16)
    tokens_here = flat_hidden.shape[0]
    top_count = route_experts.shape[-1]
    experts = ctx_count * wide_count
    capacity = max(2, 2 * tokens_here * top_count // experts)
    chosen = route_experts.reshape(-1)
    order = jnp.arange(chosen.shape[0])
    earlier = (chosen[None, :] == chosen[:, None]) & (order[None, :] < order[:, None])
    slot = jnp.sum(earlier.astype(jnp.int32), axis=1)
    target = chosen * capacity + slot
    slot_ids = jnp.arange(experts * capacity)
    select = jnp.any(
        target.reshape(tokens_here, top_count)[None, :, :] == slot_ids[:, None, None], axis=-1
    ).astype(jnp.bfloat16)
    outgoing = (
        jnp.dot(select, normed, preferred_element_type=jnp.float32)
        .astype(jnp.bfloat16)
        .reshape(experts, capacity, width)
    )
    inner = inner_weight[0]
    outer = outer_weight[0]
    returned = lax.all_to_all(
        run_expert(
            lax.all_to_all(outgoing, ("ctx", "wide"), split_axis=0, concat_axis=0, tiled=True),
            inner,
            outer,
        ),
        ("ctx", "wide"),
        split_axis=0,
        concat_axis=0,
        tiled=True,
    )
    flat_back = returned.reshape(experts * capacity, width)
    picked = flat_back[target].reshape(tokens_here, top_count, width)
    mixture = jnp.sum(
        route_weights.reshape(tokens_here, top_count, 1) * picked.astype(jnp.float32), axis=1
    )
    return (flat_hidden + mixture).reshape(hidden.shape).astype(jnp.bfloat16)


def solution(mesh):
    placed = (
        P("ctx", None, "wide"),
        P("ctx", None, "wide"),
        P("ctx", None, "wide"),
        P(),
        P(("ctx", "wide"), None, None),
        P("wide", "ctx"),
        P(),
        P(("ctx", "wide"), None, None),
        P(("ctx", "wide"), None, None),
        P(("ctx", "wide"), None, None),
        P(("ctx", "wide"), None, None),
    )
    return jax.shard_map(
        shards,
        mesh=mesh,
        in_specs=placed,
        out_specs=P(("ctx", "wide"), None, None),
        check_vma=False,
    )
```

profile of v0, /device:TPU:1, one launch (start us, length us, event | category | flops | bytes accessed | tf_op | source)
XLA Modules:
  0.0 549.8 jit_solution(6149136742900005784)
XLA Ops:
  6.5 1.7 copy.68
  8.3 0.7 all-gather.9.cloned.1.call-update
  9.0 2.1 copy.73
  11.2 1.5 copy.70
  12.7 0.2 iota_compare_fusion
  12.9 0.8 iota_compare_fusion.3
  13.6 36.3 %all-gather.5.cloned.1.call-done = bf16[2048,4,128]{0,2,1:T(8,128)(2,1)} async-done(((bf16[128,4,128]{0,2,1:T(8,128)(2,1)}), bf16[2048,4,128]{0,2,1:T(8,128)(2,1)}) %all-gather.5.cloned.1.call-update) | async-done | bytes 2097168 | tf_op jit(solution)/shard_map/all_gather | solution.py:77
  50.0 14.6 %fusion.9 = (f32[4,8,128]{2,1,0:T(8,128)S(1)}, f32[4,2048,128,8]{2,1,3,0:T(8,128)}) fusion(pred[128,2048]{0,1:T(8,128)(4,1)S(1)} %iota_compare_fusion, bf16[128,4,8,64]{0,3,2,1:T(8,128)(2,1)S(1)} %bitcast.140, bf16[2048,4,1,2,64]{0,4,3,1,2:T(8,128)(2,1)} %bitcast.142), kind=kOutput, calls=%fused_computation.13 | convolution fusion | flops 1098903552 | bytes 35405824 | tf_op jit(solution)/shard_map/tpghd,jpgd->pghtj/dot_general | solution.py:19
  64.5 22.8 %all-gather.9.cloned.1.call-done = bf16[16,180,512]{2,1,0:T(8,128)(2,1)} async-done(((bf16[1,180,512]{2,1,0:T(8,128)(2,1)}), bf16[16,180,512]{2,1,0:T(8,128)(2,1)}) %all-gather.9.cloned.1.call-update) | async-done | bytes 2949136 | tf_op jit(solution)/shard_map/all_gather | solution.py:91
  87.3 4.3 reshape.282
  91.7 49.8 %all-gather.7.cloned.1.call-done = bf16[8192,4,128]{0,2,1:T(8,128)(2,1)} async-done(((bf16[512,4,128]{0,2,1:T(8,128)(2,1)}), bf16[8192,4,128]{0,2,1:T(8,128)(2,1)}) %all-gather.7.cloned.1.call-update) | async-done | bytes 8388624 | tf_op jit(solution)/shard_map/all_gather | solution.py:81
  141.5 46.3 %fusion = (f32[4,8,128]{2,1,0:T(8,128)S(1)}, f32[4,8192,128,8]{2,1,3,0:T(8,128)}) fusion(pred[4,8192]{1,0:T(4,128)(4,1)S(1)} %iota_compare_fusion.3, bf16[128,4,8,64]{0,3,2,1:T(8,128)(2,1)S(1)} %bitcast.141, bf16[8192,4,1,2,64]{0,4,3,1,2:T(8,128)(2,1)} %bitcast.148), kind=kOutput, calls=%fused_computation.3 | convolution fusion | flops 4395626496 | bytes 138985472 | tf_op jit(solution)/shard_map/tpghd,jpgd->pghtj/dot_general | solution.py:19
  187.8 14.2 %fusion.12 = f32[4,8,128]{2,1,0:T(8,128)S(1)} fusion(f32[4,2048,128,8]{2,1,3,0:T(8,128)} %get-tuple-element.13, f32[4,8,128]{2,1,0:T(8,128)S(1)} %get-tuple-element.11, pred[128,2048]{0,1:T(8,128)(4,1)S(1)} %iota_compare_fusion), kind=kLoop, calls=%fused_computation.16 | loop fusion | flops 33550336 | bytes 33849344 | tf_op jit(solution)/shard_map/reduce_sum | solution.py:26
  202.0 41.1 %fusion.3 = f32[4,8,128]{2,1,0:T(8,128)S(1)} fusion(f32[4,8192,128,8]{2,1,3,0:T(8,128)} %get-tuple-element.15, f32[4,8,128]{2,1,0:T(8,128)S(1)} %get-tuple-element.10, pred[4,8192]{1,0:T(4,128)(4,1)S(1)} %iota_compare_fusion.3), kind=kLoop, calls=%fused_computation.6 | loop fusion | flops 134213632 | bytes 134283264 | tf_op jit(solution)/shard_map/reduce_sum | solution.py:26
  243.1 13.6 %fusion.38 = f32[4,8,128,64]{2,3,1,0:T(8,128)S(1)} fusion(f32[4,2048,128,8]{2,1,3,0:T(8,128)} %get-tuple-element.13, f32[4,8,128]{2,1,0:T(8,128)S(1)} %get-tuple-element.11, pred[128,2048]{0,1:T(8,128)(4,1)S(1)} %iota_compare_fusion, bf16[2048,4,1,2,64]{0,4,3,1,2:T(8,128)(2,1)S(1)} %bitcast.143, f32[4,8,128]{2,1,0:T(8,128)S(1)} %get-tuple-element.6, ...), kind=kOutput, calls=%fused_computation.40 | convolution fusion | flops 1107820544 | bytes 35962880 | tf_op jit(solution)/shard_map/pghtj,jpgd->pghtd/dot_general | solution.py:27
  256.7 44.8 %divide_convert_fusion = bf16[4,8,128,64]{2,3,1,0:T(8,128)(2,1)S(1)} fusion(f32[4,8,128,64]{2,3,1,0:T(8,128)S(1)} %fusion.38, f32[4,8192,128,8]{2,1,3,0:T(8,128)} %get-tuple-element.15, f32[4,8,128]{2,1,0:T(8,128)S(1)} %get-tuple-element.10, pred[4,8192]{1,0:T(4,128)(4,1)S(1)} %iota_compare_fusion.3, bf16[8192,4,1,2,64]{0,4,3,1,2:T(8,128)(2,1)} %bitcast.149, ...), kind=kOutput, calls=%fused_computation.44 | convolution fusion | flops 4429971456 | bytes 140050432 | tf_op jit(solution)/shard_map/pghtj,jpgd->pghtd/dot_general | solution.py:27
  301.5 3.5 convolution_convert_fusion.1
  305.1 0.1 copy.81
  305.2 0.1 eq.28
  305.3 0.2 convert_reduce_fusion
  305.5 0.1 reduce_sum.54
  305.7 0.1 copy.80
  305.9 0.1 fusion.45
  306.0 78.0 %reduce-scatter.2.cloned.1.call-done = bf16[16,4,2880]{2,0,1:T(8,128)(2,1)} async-done(((bf16[128,4,2880]{2,0,1:T(8,128)(2,1)}), bf16[16,4,2880]{2,0,1:T(8,128)(2,1)}) %reduce-scatter.2.cloned.1.call-update) | async-done | bytes 368656 | tf_op jit(solution)/shard_map/reduce_scatter | solution.py:98
  384.0 1.2 multiply_reduce_fusion.1
  385.2 0.3 copy.83
  385.5 1.1 reshape.262
  386.9 2.2 convolution_convert_fusion
  389.0 3.0 copy.85
  392.0 4.7 reshape.263
  396.7 47.2 %all_to_all.10 = bf16[128,4,2880]{2,1,0:T(4,128)(2,1)} all-to-all(bf16[128,4,2880]{2,1,0:T(4,128)(2,1)S(1)} %reshape.263), channel_id=1, replica_groups=mesh['ctx'=16,'wide'=8] {'ctx','wide'}, dimensions={0} | all-to-all | bytes 5898240 | tf_op jit(solution)/shard_map/all_to_all | solution.py:131
  443.9 4.4 reshape.264
  448.3 15.3 %fusion.14 = f32[512,2880]{0,1:T(8,128)} fusion(bf16[512,2880]{1,0:T(8,128)(2,1)S(1)} %reshape.264, bf16[1,2880,2880]{2,1,0:T(8,128)(2,1)} %param.20), kind=kOutput, calls=%fused_computation.18 | convolution fusion | flops 8493465600 | bytes 25436160 | tf_op jit(solution)/shard_map/dot_general | solution.py:47
  463.6 11.7 %fusion.22 = bf16[512,2880]{0,1:T(8,128)(2,1)} fusion(bf16[1,1440,2880]{2,1,0:T(8,128)(2,1)} %param.21, f32[512,2880]{0,1:T(8,128)} %fusion.14), kind=kOutput, calls=%fused_computation.25 | convolution fusion | flops 4254105600 | bytes 17141760 | tf_op jit(solution)/shard_map/dot_general | solution.py:52
  475.3 3.3 copy.86
  478.7 2.4 reshape.265
  481.1 7.3 %all-to-all-start.1 = ((bf16[128,4,2880]{2,1,0:T(4,128)(2,1)}), bf16[128,4,2880]{2,1,0:T(4,128)(2,1)}, u32[]{:S(2)}, u32[]{:S(2)}) async-start(bf16[128,4,2880]{2,1,0:T(4,128)(2,1)} %reshape.265), calls=%async_computation.2 | async-start | bytes 6029312 | tf_op jit(solution)/shard_map/all_to_all | solution.py:129
  488.5 0.1 copy.87
  488.6 0.1 mul.142
  488.7 0.1 copy.97
  488.8 38.0 %all-to-all-done.1 = bf16[128,4,2880]{2,1,0:T(4,128)(2,1)} async-done(((bf16[128,4,2880]{2,1,0:T(4,128)(2,1)}), bf16[128,4,2880]{2,1,0:T(4,128)(2,1)}, u32[]{:S(2)}, u32[]{:S(2)}) %all-to-all-start.1) | async-done | bytes 2949152 | tf_op jit(solution)/shard_map/all_to_all | solution.py:129
  526.8 4.4 reshape.266
  531.2 2.7 gather_fusion
  533.9 2.8 reshape.267
  536.7 2.9 multiply_reduce_fusion
  539.6 1.3 reduce_sum.58
  540.9 1.1 fusion.44
  542.0 0.9 copy.89
  (31 shorter events, 0.6 us)
Async XLA Ops:
  6.5 43.4 %all-gather.5.cloned.1.call-start = ((), (), s32[]{:S(2)}) async-start(), calls=%async_computation.3 | async-start | bytes 2228224 | tf_op jit(solution)/shard_map/all_gather | solution.py:77
  8.2 79.1 %all-gather.9.cloned.1.call-start = ((), (), s32[]{:S(2)}) async-start(), calls=%async_computation.6 | async-start | bytes 3203072 | tf_op jit(solution)/shard_map/all_gather | solution.py:91
  9.0 132.5 %all-gather.7.cloned.1.call-start = ((), (), s32[]{:S(2)}) async-start(), calls=%async_computation.4 | async-start | bytes 8912896 | tf_op jit(solution)/shard_map/all_gather | solution.py:81
  11.2 372.9 %reduce-scatter.2.cloned.1.call-start = ((), (), s32[]{:S(2)}) async-start(), calls=%async_computation.5 | async-start | bytes 3391488 | tf_op jit(solution)/shard_map/reduce_scatter | solution.py:98
  202.0 41.1 %copy-start.2 = (bf16[2048,4,128]{0,2,1:T(8,128)(2,1)S(1)}, bf16[2048,4,128]{0,2,1:T(8,128)(2,1)}, u32[]{:S(2)}) copy-start(bf16[2048,4,128]{0,2,1:T(8,128)(2,1)} %all-gather.5.cloned.1.call-done) | copy-start | bytes 6291460
  256.7 44.8 %copy-start = (bf16[2880,512,1]{1,0,2:T(8,128)(2,1)S(1)}, bf16[2880,512,1]{1,0,2:T(8,128)(2,1)}, u32[]{:S(2)}) copy-start(bf16[2880,512,1]{1,0,2:T(8,128)(2,1)} %reshape.282) | copy-start | bytes 8847364
  301.5 3.6 copy-start.3
  301.5 82.5 %copy-start.1 = (bf16[16,4,2880]{2,1,0:T(4,128)(2,1)S(1)}, bf16[16,4,2880]{2,1,0:T(4,128)(2,1)}, u32[]{:S(2)}) copy-start(bf16[16,4,2880]{2,1,0:T(4,128)(2,1)} %param.15) | copy-start | bytes 1105924
  301.5 85.3 %copy-start.4 = (f32[2880]{0:T(1024)S(1)}, f32[2880]{0:T(1024)}, u32[]{:S(2)}) copy-start(f32[2880]{0:T(1024)} %param.17) | copy-start | bytes 34564
  475.3 13.3 %copy-start.5 = (f32[16,4,4]{0,2,1:T(4,128)S(1)}, f32[16,4,4]{0,2,1:T(4,128)}, u32[]{:S(2)}) copy-start(f32[16,4,4]{0,2,1:T(4,128)} %param.19) | copy-start | bytes 3076
  481.1 45.7 %all-to-all-start.1 = ((bf16[128,4,2880]{2,1,0:T(4,128)(2,1)}), bf16[128,4,2880]{2,1,0:T(4,128)(2,1)}, u32[]{:S(2)}, u32[]{:S(2)}) async-start(bf16[128,4,2880]{2,1,0:T(4,128)(2,1)} %reshape.265), calls=%async_computation.2 | async-start | bytes 6029312 | tf_op jit(solution)/shard_map/all_to_all | solution.py:129
Sparse Core Ops, SparseCore 0:
  9.0 40.9 all-gather.4
  51.7 35.6 all-gather.8
  89.0 52.4 all-gather.6
  305.2 78.8 reduce-scatter.1
where the time goes:
time: 559 us; the launch traced here: 550 us
  waiting for transfers between devices  226 us (40%)
  matrix products  152 us (27%)
  other arithmetic  61.7 us (11%)
  blocking collectives  47.2 us (8%)
  local copies, waits for them, and re-layouts  42 us (8%)
  between operations  13.8 us (2%)
  starting transfers between devices  7.47 us (1%)
    reduce_scatter x1, waiting for transfers between devices, shards(): lax.psum_scatter(product.reshape(count, prompts, -1).astype(jnp.bfloat16)...  78 us
    dot_general x2, matrix products, absorb(): jnp.einsum('tpghd,jpgd->pghtj', query_block, keys, preferred_element_type...  60.9 us
    dot_general x2, matrix products, absorb(): jnp.einsum('pghtj,jpgd->pghtd', weights.astype(jnp.bfloat16), values, pre...  58.4 us
    reduce_sum x2, other arithmetic, absorb(): total = total * decay + jnp.sum(weights, axis=-1)  55.3 us
    all_gather x1, waiting for transfers between devices, shards(): piece = lax.all_gather(cached_entries, 'ctx', axis=0, tiled=True)  49.8 us
    all_to_all x1, blocking collectives, shards(): lax.all_to_all(outgoing, ('ctx', 'wide'), split_axis=0, concat_axis=0, ti...  47.2 us
    all_to_all x1, waiting for transfers between devices, shards(): lax.all_to_all(run_expert(lax.all_to_all(outgoing, ('ctx', 'wide'), split...  38 us
    all_gather x1, waiting for transfers between devices, shards(): recent = lax.all_gather(new_entries, 'ctx', axis=0, tiled=True)  36.3 us
  transfers between devices with their start and end apart: 5, of which 5 were waited for; matrix products, arithmetic and copies ran while one was open for 4% of the time, Pallas kernels for 0%

commit v1 on v0

v1 whole, which is shorter than its diff:
```python
import functools
import jax
import jax.numpy as jnp
from jax import lax
from jax.experimental import pallas as pl
from jax.experimental.pallas import tpu as pltpu
from jax.sharding import PartitionSpec as P

HEAD_DIM = 64
LANES = 128
NEGATIVE = -1e30


def attend_kernel(info_ref, q_ref, kv_ref, out_ref, rows_ref, cached_ref, recent_ref, score_ref, best_ref, accum_ref,
                  *, base, own, cached, tile, block):
    ctx_count = kv_ref.shape[0]
    tokens = q_ref.shape[0]
    recent = own * ctx_count
    per_block, per_recent = block // cached, block // own
    cached_blocks, recent_blocks = cached * ctx_count // block, recent // block
    length = info_ref[base + pl.program_id(0)]
    first = info_ref[info_ref.shape[0] - 1] * tokens
    pairs = q_ref.shape[1] // LANES
    low = lax.broadcasted_iota(jnp.int32, (tokens, LANES), 1) < HEAD_DIM
    for pair in range(pairs):
        both = q_ref[:, pair * LANES:(pair + 1) * LANES].astype(jnp.float32) * 0.125
        for odd in range(2):
            head = pltpu.roll(both, HEAD_DIM, 1) if odd else both
            rows_ref[pl.ds((2 * pair + odd) * tokens, tokens)] = jnp.where(low, head, 0.0).astype(jnp.bfloat16)
    def ones_beside(entries):
        lane = lax.broadcasted_iota(jnp.int32, entries.shape, 1)
        return jnp.where(lane < HEAD_DIM, 1.0, entries.astype(jnp.float32)).astype(jnp.bfloat16)

    @pl.loop(0, ctx_count)
    def _(c):
        cached_ref[pl.ds(c * cached, cached)] = ones_beside(kv_ref[c, :cached])
        recent_ref[pl.ds(c * own, own)] = ones_beside(kv_ref[c, cached:])

    whole = length // block
    rest = length - whole * block

    for start in range(0, rows_ref.shape[0], tile):
        rows = rows_ref[start:start + tile]

        def scores_of(keys):
            return lax.dot_general(rows, keys, (((1,), (1,)), ((), ())), preferred_element_type=jnp.float32)

        def cached_keys(b):
            return kv_ref[pl.ds(b * per_block, per_block), :cached].reshape(block, LANES)

        def keep(slot, scores):
            score_ref[slot] = scores
            best = best_ref[...]
            for part in range(0, block, LANES):
                best = jnp.maximum(best, scores[:, part:part + LANES])
            best_ref[...] = best

        best_ref[...] = jnp.full(best_ref.shape, NEGATIVE, jnp.float32)
        column = lax.broadcasted_iota(jnp.int32, (tile, block), 1)
        for b in range(recent_blocks):
            token = start + lax.broadcasted_iota(jnp.int32, (tile, block), 0)
            token = first + lax.rem(token, tokens)
            keys = kv_ref[b * per_recent:(b + 1) * per_recent, cached:].reshape(block, LANES)
            keep(cached_blocks + b, jnp.where(column + b * block <= token, scores_of(keys), NEGATIVE))

        @pl.loop(0, whole)
        def _(b):
            keep(b, scores_of(cached_keys(b)))

        @pl.when(rest > 0)
        def _():
            keep(whole, jnp.where(column < rest, scores_of(cached_keys(whole)), NEGATIVE))

        best_ref[...] = jnp.broadcast_to(jnp.max(best_ref[...], axis=1, keepdims=True), best_ref.shape)
        accum_ref[...] = jnp.zeros(accum_ref.shape, jnp.float32)

        def weigh(slot, entries):
            best = best_ref[...]
            probs = [
                jnp.exp(score_ref[slot, :, part:part + LANES] - best).astype(jnp.bfloat16)
                for part in range(0, block, LANES)
            ]
            accum_ref[...] += jnp.dot(jnp.concatenate(probs, axis=1), entries, preferred_element_type=jnp.float32)

        for b in range(recent_blocks):
            weigh(cached_blocks + b, recent_ref[b * block:(b + 1) * block])

        @pl.loop(0, (length + block - 1) // block)
        def _(b):
            weigh(b, cached_ref[pl.ds(pl.multiple_of(b * block, block), block)])

        accum = accum_ref[...]
        done = accum / pltpu.roll(accum, HEAD_DIM, 1)
        for at in range(start, start + tile, 2 * tokens):
            even = done[at - start:at - start + tokens]
            odd = done[at - start + tokens:at - start + 2 * tokens]
            pair = at // (2 * tokens)
            out_ref[:, pair * LANES:(pair + 1) * LANES] = jnp.where(low, pltpu.roll(even, HEAD_DIM, 1), odd).astype(jnp.bfloat16)


def attend(info, queries, entries, base, prompts, own, tile=512, block=1024):
    _, tokens, width = queries.shape
    _, ctx_count, held, _ = entries.shape
    cached = held - own
    rows = tokens * width // HEAD_DIM
    slots = ctx_count * held // block
    return pl.pallas_call(
        functools.partial(attend_kernel, base=base, own=own, cached=cached, tile=tile, block=block),
        out_shape=jax.ShapeDtypeStruct((prompts, tokens, width), jnp.bfloat16),
        grid=(prompts,),
        in_specs=[
            pl.BlockSpec(memory_space=pltpu.SMEM),
            pl.BlockSpec((None, tokens, width), lambda p: (base + p, 0, 0)),
            pl.BlockSpec((None, ctx_count, held, LANES), lambda p: (base + p, 0, 0, 0)),
        ],
        out_specs=pl.BlockSpec((None, tokens, width), lambda p: (p, 0, 0)),
        scratch_shapes=[
            pltpu.VMEM((rows, LANES), jnp.bfloat16),
            pltpu.VMEM((ctx_count * cached, LANES), jnp.bfloat16),
            pltpu.VMEM((ctx_count * own, LANES), jnp.bfloat16),
            pltpu.VMEM((slots, tile, block), jnp.float32),
            pltpu.VMEM((tile, LANES), jnp.float32),
            pltpu.VMEM((tile, LANES), jnp.float32),
        ],
        compiler_params=pltpu.CompilerParams(vmem_limit_bytes=46 * 2**20),
        cost_estimate=pl.CostEstimate(
            flops=8 * prompts * rows * ctx_count * held * HEAD_DIM,
            bytes_accessed=prompts * ctx_count * held * 2 * LANES,
            transcendentals=prompts * rows * ctx_count * held,
        ),
    )(info, queries, entries)


def project_kernel(attended_ref, weight_ref, out_ref, *, step):
    prompts, tokens, depth = attended_ref.shape
    members, _, width = out_ref.shape
    each = tokens // members
    attended = attended_ref[...].reshape(prompts * tokens, depth)
    for at in range(0, width, step):
        size = min(step, width - at)
        product = lax.dot_general(
            attended, weight_ref[at:at + size], (((1,), (1,)), ((), ())), preferred_element_type=jnp.float32
        ).astype(jnp.bfloat16)
        for prompt in range(prompts):
            out_ref[:, prompt * each:(prompt + 1) * each, at:at + size] = product[
                prompt * tokens:(prompt + 1) * tokens
            ].reshape(members, each, size)


def project(attended, weight, members, step=512):
    prompts, tokens, depth = attended.shape
    width = weight.shape[0]
    return pl.pallas_call(
        functools.partial(project_kernel, step=step),
        out_shape=jax.ShapeDtypeStruct((members, prompts * tokens // members, width), jnp.bfloat16),
        in_specs=[pl.BlockSpec(memory_space=pltpu.VMEM)] * 2,
        out_specs=pl.BlockSpec(memory_space=pltpu.VMEM),
        compiler_params=pltpu.CompilerParams(vmem_limit_bytes=24 * 2**20),
        cost_estimate=pl.CostEstimate(
            flops=2 * prompts * tokens * width * depth,
            bytes_accessed=2 * (weight.size + prompts * tokens * (depth + width)),
            transcendentals=0,
        ),
    )(attended, weight)


def pick_kernel(select_ref, rows_ref, out_ref, *, step):
    width = rows_ref.shape[1]
    for at in range(0, width, step):
        size = min(step, width - at)
        out_ref[:, at:at + size] = jnp.dot(
            select_ref[...], rows_ref[:, at:at + size], preferred_element_type=jnp.float32
        ).astype(jnp.bfloat16)


def pick(select, rows, step=512):
    return pl.pallas_call(
        functools.partial(pick_kernel, step=step),
        out_shape=jax.ShapeDtypeStruct((select.shape[0], rows.shape[1]), jnp.bfloat16),
        in_specs=[pl.BlockSpec(memory_space=pltpu.VMEM)] * 2,
        out_specs=pl.BlockSpec(memory_space=pltpu.VMEM),
        compiler_params=pltpu.CompilerParams(vmem_limit_bytes=24 * 2**20),
        cost_estimate=pl.CostEstimate(
            flops=2 * select.size * rows.shape[1], bytes_accessed=2 * select.shape[0] * rows.shape[1], transcendentals=0
        ),
    )(select, rows)


GROUP = 2


def exchange(value, axis):
    return lax.ppermute(value, axis, [(0, 1), (1, 0)])


ROWS = 64


def expert_kernel(rows_ref, inner_ref, outer_ref, out_ref, first_ref, second_ref, lifted_ref, active_ref, sems, *, step):
    count, width = rows_ref.shape
    half = outer_ref.shape[0]
    bounds = [(at, min(step, width - at)) for at in range(0, width, step)]
    lifts = [
        pltpu.make_async_copy(inner_ref.at[pl.ds(at, size)], first_ref.at[pl.ds(at, size)], sems.at[index])
        for index, (at, size) in enumerate(bounds)
    ]
    lowering = pltpu.make_async_copy(outer_ref, second_ref, sems.at[len(bounds)])
    for copy in lifts + [lowering]:
        copy.start()
    whole = width // step
    tail = width - whole * step

    def over_columns(body):
        @pl.loop(0, whole)
        def _(n):
            body(pl.ds(pl.multiple_of(n * step, step), step))

        if tail:
            body(pl.ds(whole * step, tail))

    for index, (at, size) in enumerate(bounds):
        lifts[index].wait()

        def lift(columns, at=at, size=size, index=index):
            part = jnp.dot(rows_ref[:, at:at + size], first_ref[at:at + size, columns], preferred_element_type=jnp.float32)
            if index:
                lifted_ref[:, columns] += part
            else:
                lifted_ref[:, columns] = part

        over_columns(lift)

    @pl.loop(0, count // ROWS)
    def _(r):
        some = pl.ds(pl.multiple_of(r * ROWS, ROWS), ROWS)
        gate = lifted_ref[some, :half]
        upper = lifted_ref[some, half:]
        sigmoid = 0.5 + 0.5 * jnp.tanh(0.851 * gate)
        active_ref[some] = ((upper + 1.0) * gate * sigmoid).astype(jnp.bfloat16)

    lowering.wait()

    def lower(columns):
        out_ref[:, columns] = jnp.dot(
            active_ref[...], second_ref[:, columns], preferred_element_type=jnp.float32
        ).astype(jnp.bfloat16)

    over_columns(lower)


def run_expert(rows, inner, outer, step=1536):
    count, width = rows.shape
    return pl.pallas_call(
        functools.partial(expert_kernel, step=step),
        out_shape=jax.ShapeDtypeStruct(rows.shape, jnp.bfloat16),
        in_specs=[
            pl.BlockSpec(memory_space=pltpu.VMEM),
            pl.BlockSpec(memory_space=pl.ANY),
            pl.BlockSpec(memory_space=pl.ANY),
        ],
        out_specs=pl.BlockSpec(memory_space=pltpu.VMEM),
        scratch_shapes=[
            pltpu.VMEM(inner.shape, jnp.bfloat16),
            pltpu.VMEM(outer.shape, jnp.bfloat16),
            pltpu.VMEM((count, inner.shape[1]), jnp.float32),
            pltpu.VMEM((count, outer.shape[0]), jnp.bfloat16),
            pltpu.SemaphoreType.DMA((-(-width // step) + 1,)),
        ],
        compiler_params=pltpu.CompilerParams(vmem_limit_bytes=50 * 2**20),
        cost_estimate=pl.CostEstimate(
            flops=2 * count * (inner.size + outer.size), bytes_accessed=2 * (inner.size + outer.size), transcendentals=0
        ),
    )(rows, inner, outer)


def slots_of(experts, core, wide_count, capacity, block):
    chosen = experts.reshape(-1)
    order = jnp.arange(chosen.shape[0])
    earlier = (chosen[None, :] == chosen[:, None]) & (order[None, :] < order[:, None])
    rank = jnp.sum(earlier.astype(jnp.int32), axis=1)
    chip = (chosen // (2 * wide_count)) * wide_count + chosen % wide_count
    here = (chosen // wide_count) % 2 == core
    return jnp.where(here, chip * (2 * capacity) + block * capacity + rank, -1).reshape(experts.shape)


def shards(
    queries,
    new_entries,
    cached_entries,
    cache_lengths,
    residual,
    out_weight,
    norm_gain,
    route_experts,
    route_weights,
    inner_weight,
    outer_weight,
):
    tokens, prompts, query_width = queries.shape
    owned, _, width = residual.shape
    members = lax.axis_size("wide")
    chips = lax.axis_size("zlo") * lax.axis_size("x") * members
    core = lax.axis_index("core")
    ctx = (lax.axis_index("zlo") * lax.axis_size("x") + lax.axis_index("x")) * 2 + core
    info = jnp.concatenate([cache_lengths, ctx.astype(jnp.int32)[None]])
    top = route_experts.shape[-1]

    experts = route_experts.transpose(1, 0, 2).reshape(-1, top)
    weights = route_weights.transpose(1, 0, 2).reshape(-1, top)
    here = experts.shape[0]
    capacity = 4
    slots = jnp.concatenate(
        [
            slots_of(experts, core, members, capacity, 0),
            slots_of(exchange(experts, "core"), core, members, capacity, 1),
        ]
    )
    shares = jnp.concatenate([weights, exchange(weights, "core")])
    slot_ids = jnp.arange(chips * 2 * capacity)
    match = slots[:, :, None] == slot_ids[None, None, :]
    select = jnp.any(match, axis=1).T.astype(jnp.bfloat16)

    entries = jnp.concatenate([cached_entries, new_entries], axis=0).transpose(1, 0, 2)
    held = lax.all_gather(entries, ("zlo", "x", "core"), axis=1, tiled=False)
    out_weight, held = lax.optimization_barrier((out_weight, held))
    full_weight = lax.all_gather(out_weight.T, ("zlo", "x", "core"), axis=0, tiled=True)
    stretch = queries.transpose(1, 0, 2)
    parts = []
    for base in range(0, prompts, GROUP):
        attended = attend(info, stretch, held, base, GROUP, tokens)
        product = project(attended, full_weight, members)
        parts.append(lax.all_to_all(product, "wide", split_axis=0, concat_axis=0, tiled=True))
    projected = jnp.concatenate([jnp.sum(part.astype(jnp.float32), axis=0) for part in parts])
    hidden = residual.transpose(1, 0, 2).reshape(-1, width).astype(jnp.float32) + projected

    scale = lax.rsqrt(jnp.mean(hidden * hidden, axis=-1, keepdims=True) + 1e-05)
    normed = (hidden * scale * norm_gain[None, :]).astype(jnp.bfloat16)
    both = jnp.concatenate([normed, exchange(normed, "core")])
    outgoing = pick(select, both)
    outgoing, shares, match = lax.optimization_barrier((outgoing, shares, match))
    share = jnp.sum(jnp.where(match, shares[:, :, None], 0.0), axis=1)
    share_high = share.astype(jnp.bfloat16)
    share_low = (share - share_high.astype(jnp.float32)).astype(jnp.bfloat16)

    def across(rows):
        swapped = lax.all_to_all(
            rows.reshape(chips, 2 * capacity, width), ("zlo", "x", "wide"), split_axis=0, concat_axis=0, tiled=True
        )
        return swapped.reshape(rows.shape)

    returned = across(run_expert(across(outgoing), inner_weight[0], outer_weight[0]))
    mixture = jnp.dot(share_high, returned, preferred_element_type=jnp.float32) + jnp.dot(
        share_low, returned, preferred_element_type=jnp.float32
    )
    others = exchange(mixture[here:].astype(jnp.bfloat16), "core").astype(jnp.float32)
    layer_out = (hidden + (mixture[:here] + others)).astype(jnp.bfloat16)
    return layer_out.reshape(prompts, owned, width).transpose(1, 0, 2)


def solution(mesh):
    ctx_count, wide_count = mesh.devices.shape
    split = jax.sharding.Mesh(
        mesh.devices.reshape(2, ctx_count // 4, 2, wide_count), ("zlo", "x", "core", "wide")
    )
    ctx = ("zlo", "x", "core")
    every = ctx + ("wide",)
    placed = (
        P(ctx, None, "wide"),
        P(ctx, None, "wide"),
        P(ctx, None, "wide"),
        P(),
        P(every, None, None),
        P("wide", ctx),
        P(),
        P(every, None, None),
        P(every, None, None),
        P(every, None, None),
        P(every, None, None),
    )
    return jax.shard_map(
        shards,
        mesh=split,
        in_specs=placed,
        out_specs=P(every, None, None),
        check_vma=False,
    )
```

time: 559 us -> 334 us (0.60); the launches traced: 550 us -> 331 us
  matrix products: 152 us -> 3.69 us
  waiting for transfers between devices: 226 us -> 136 us
  Pallas kernels: 0 us -> 75.2 us
  other arithmetic: 61.7 us -> 8.59 us
  starting transfers between devices: 7.47 us -> 26.9 us
  local copies, waits for them, and re-layouts: 42 us -> 23.3 us
    dot_general x8 -> x2, matrix products: 152 us -> 3.69 us  [the longest x1 2.33 us: shards(): jnp.dot(share_high, returned, preferred_element_type=jnp.float32)]
    reduce_scatter x1 -> x0, waiting for transfers between devices: 78 us -> none  [shards(): lax.psum_scatter(product.reshape(count, prompts, -1).astype(jnp.bfloat16)...]
    pallas_call x0 -> x6, Pallas kernels: none -> 75.2 us  [the longest x2 47.1 us: attend(): pl.pallas_call(functools.partial(attend_kernel, base=base, own=own, cache...]
    reduce_sum x5 -> x6, other arithmetic: 59.5 us -> 4.48 us  [the longest x1 1.89 us: shards(): share = jnp.sum(jnp.where(match, shares[:, :, None], 0.0), axis=1)]
    all_gather x3 -> x2, waiting for transfers between devices: 109 us -> 83 us  [the longest x1 65.7 us: shards(): held = lax.all_gather(entries, ('zlo', 'x', 'core'), axis=1, tiled=False)]
    reshape x5 -> x2, local copies, waits for them, and re-layouts: 17 us -> 0.97 us  [the longest x1 0.89 us: shards(): return layer_out.reshape(prompts, owned, width).transpose(1, 0, 2)]
    all_to_all x1 -> x3, waiting for transfers between devices: 38 us -> 53.2 us  [the longest x1 33.5 us: across(): lax.all_to_all(rows.reshape(chips, 2 * capacity, width), ('zlo', 'x', 'wi...]
    all_to_all x1 -> x3, starting transfers between devices: 7.34 us -> 21.2 us  [the longest x2 13.4 us: shards(): lax.all_to_all(product, 'wide', split_axis=0, concat_axis=0, tiled=True)]
  transfers between devices with their start and end apart: 5 -> 9, of which waited for: 5 -> 4; matrix products, arithmetic and copies ran while one was open for 4% -> 3% of each run, Pallas kernels for 0% -> 15%
where the time goes in v1:
time: 334 us; the launch traced here: 331 us
  waiting for transfers between devices  136 us (41%)
  Pallas kernels  75.2 us (23%)
  blocking collectives  43.3 us (13%)
  starting transfers between devices  26.9 us (8%)
  local copies, waits for them, and re-layouts  23.3 us (7%)
  between operations  13.8 us (4%)
  other arithmetic  8.59 us (3%)
  matrix products  3.69 us (1%)
    all_gather x1, waiting for transfers between devices, shards(): held = lax.all_gather(entries, ('zlo', 'x', 'core'), axis=1, tiled=False)  65.7 us
    pallas_call x2, Pallas kernels, attend(): pl.pallas_call(functools.partial(attend_kernel, base=base, own=own, cache...  47.1 us
    all_to_all x1, blocking collectives, across(): lax.all_to_all(rows.reshape(chips, 2 * capacity, width), ('zlo', 'x', 'wi...  43.3 us
    all_to_all x1, waiting for transfers between devices, across(): lax.all_to_all(rows.reshape(chips, 2 * capacity, width), ('zlo', 'x', 'wi...  33.5 us
    pallas_call x1, Pallas kernels, run_expert(): pl.pallas_call(functools.partial(expert_kernel, step=step), out_shape=jax...  25 us
    all_to_all x2, waiting for transfers between devices, shards(): lax.all_to_all(product, 'wide', split_axis=0, concat_axis=0, tiled=True)  19.8 us
    all_gather x1, waiting for transfers between devices, shards(): lax.all_gather(out_weight.T, ('zlo', 'x', 'core'), axis=0, tiled=True)  17.3 us
    all_to_all x2, starting transfers between devices, shards(): lax.all_to_all(product, 'wide', split_axis=0, concat_axis=0, tiled=True)  13.4 us
  transfers between devices with their start and end apart: 9, of which 4 were waited for; matrix products, arithmetic and copies ran while one was open for 3% of the time, Pallas kernels for 15%

profile of v1, /device:TPU:1, one launch (start us, length us, event | category | flops | bytes accessed | tf_op | source)
XLA Modules:
  0.0 331.1 jit_solution(3383804968981611513)
XLA Ops:
  6.5 2.4 maximum_bitcast_fusion
  9.0 65.7 %all-gather.5.cloned.1.call-done = bf16[4,10240,128]{2,0,1:T(4,128)(2,1)} async-done(((bf16[4,640,128]{2,0,1:T(4,128)(2,1)}), bf16[4,10240,128]{2,0,1:T(4,128)(2,1)}) %all-gather.5.cloned.1.call-update) | async-done | bytes 10485776 | tf_op jit(solution)/shard_map/all_gather | solution.py:324
  74.8 10.7 %copy.67 = bf16[4,10240,128]{2,1,0:T(8,128)(2,1)} copy(bf16[4,10240,128]{2,0,1:T(4,128)(2,1)} %all-gather.5.cloned.1.call-done) | data formatting | bytes 20971520 | tf_op jit(solution)/shard_map/all_gather | solution.py:324
  85.8 18.2 %shard_map.109.attended_ref = bf16[2,128,512]{2,1,0:T(8,128)(2,1)S(1)} custom-call(s32[5]{0:T(128)S(1)} %pad_add_fusion.1.info_ref, bf16[4,128,512]{2,1,0:T(8,128)(2,1)S(1)} %bitcast.45, bf16[4,16,640,128]{3,2,1,0:T(8,128)(2,1)} %bitcast.47), custom_call_target="tpu_custom_call" | custom-call | flops 10737418240 | bytes 5242880 | tf_op jit(solution)/shard_map/pallas_call | solution.py:107
  104.0 0.7 copy-done.2
  104.7 17.3 %all-gather.7.cloned.1.call-done = bf16[16,180,512]{2,1,0:T(8,128)(2,1)} async-done(((bf16[1,180,512]{2,1,0:T(8,128)(2,1)}), bf16[16,180,512]{2,1,0:T(8,128)(2,1)}) %all-gather.7.cloned.1.call-update) | async-done | bytes 2949136 | tf_op jit(solution)/shard_map/all_gather | solution.py:326
  122.0 2.8 reshape.62.weight_ref
  124.8 0.9 copy-done.3
  125.7 1.1 shard_map.110
  126.8 1.2 copy-done.1
  128.0 6.5 %all-to-all-start = ((bf16[8,32,2880]{2,1,0:T(8,128)(2,1)}), bf16[8,32,2880]{2,1,0:T(8,128)(2,1)}, u32[]{:S(2)}, u32[]{:S(2)}) async-start(bf16[8,32,2880]{2,1,0:T(8,128)(2,1)} %copy-done.1), calls=%async_computation | async-start | bytes 3014656 | tf_op jit(solution)/shard_map/all_to_all | solution.py:332
  134.6 0.6 collective-permute-start
  135.3 0.2 collective-permute-start.2
  135.5 0.1 copy.69
  135.6 0.1 eq.62
  135.7 0.2 convert_reduce_fusion.3
  135.9 0.1 reduce_sum.61
  136.1 28.9 %shard_map.111.attended_ref = bf16[2,128,512]{2,1,0:T(8,128)(2,1)S(1)} custom-call(s32[5]{0:T(128)S(1)} %pad_add_fusion.1.info_ref, bf16[4,128,512]{2,1,0:T(8,128)(2,1)S(1)} %bitcast.46, bf16[4,16,640,128]{3,2,1,0:T(8,128)(2,1)} %bitcast.48), custom_call_target="tpu_custom_call" | custom-call | flops 10737418240 | bytes 5242880 | tf_op jit(solution)/shard_map/pallas_call | solution.py:107
  165.0 1.1 shard_map.112
  166.1 1.1 copy-done
  167.2 6.9 %all-to-all-start.1 = ((bf16[8,32,2880]{2,1,0:T(8,128)(2,1)}), bf16[8,32,2880]{2,1,0:T(8,128)(2,1)S(1)}, u32[]{:S(2)}, u32[]{:S(2)}) async-start(bf16[8,32,2880]{2,1,0:T(8,128)(2,1)} %copy-done), calls=%async_computation.1 | async-start | bytes 3014656 | tf_op jit(solution)/shard_map/all_to_all | solution.py:332
  174.3 0.1 copy.71
  174.4 0.1 eq.67
  174.5 0.2 convert_reduce_fusion.2
  174.7 0.1 reduce_sum.63
  175.0 1.6 convert_reduce_fusion.1
  176.6 19.8 %all-to-all-done.1 = bf16[8,32,2880]{2,1,0:T(8,128)(2,1)S(1)} async-done(((bf16[8,32,2880]{2,1,0:T(8,128)(2,1)}), bf16[8,32,2880]{2,1,0:T(8,128)(2,1)S(1)}, u32[]{:S(2)}, u32[]{:S(2)}) %all-to-all-start.1) | async-done | bytes 1474592 | tf_op jit(solution)/shard_map/all_to_all | solution.py:332
  196.4 0.2 convert_reduce_fusion
  196.7 0.4 fusion.4
  197.2 0.1 multiply_convert_fusion
  197.4 0.9 collective-permute-start.1
  198.3 1.0 iota_compare_fusion
  199.3 0.2 copy.73
  199.7 0.9 shard_map.113
  200.6 43.3 %all_to_all.20 = bf16[64,8,2880]{2,1,0:T(8,128)(2,1)} all-to-all(bf16[64,8,2880]{2,1,0:T(8,128)(2,1)S(1)} %bitcast.44), channel_id=1, replica_groups=mesh['zlo'=2,'x'=4,'core'=2,'wide'=8] {'zlo','x','wide'}, dimensions={0} | all-to-all | bytes 5898240 | tf_op jit(solution)/shard_map/all_to_all | solution.py:346
  243.9 25.0 %shard_map.114 = bf16[512,2880]{1,0:T(8,128)(2,1)} custom-call(bf16[512,2880]{1,0:T(8,128)(2,1)} %bitcast.50, bf16[2880,2880]{1,0:T(8,128)(2,1)} %bitcast.57, bf16[1440,2880]{1,0:T(8,128)(2,1)} %bitcast.58), custom_call_target="tpu_custom_call" | custom-call | flops 12740198400 | bytes 24883200 | tf_op jit(solution)/shard_map/pallas_call | solution.py:253
  268.9 7.8 %all-to-all-start.3 = ((bf16[64,8,2880]{2,1,0:T(8,128)(2,1)}), bf16[64,8,2880]{2,1,0:T(8,128)(2,1)S(1)}, u32[]{:S(2)}, u32[]{:S(2)}) async-start(bf16[64,8,2880]{2,1,0:T(8,128)(2,1)} %bitcast.16), calls=%async_computation.3 | async-start | bytes 6029312 | tf_op jit(solution)/shard_map/all_to_all | solution.py:346
  276.7 1.9 select_reduce_fusion
  278.6 33.5 %all-to-all-done.3 = bf16[64,8,2880]{2,1,0:T(8,128)(2,1)S(1)} async-done(((bf16[64,8,2880]{2,1,0:T(8,128)(2,1)}), bf16[64,8,2880]{2,1,0:T(8,128)(2,1)S(1)}, u32[]{:S(2)}, u32[]{:S(2)}) %all-to-all-start.3) | async-done | bytes 2949152 | tf_op jit(solution)/shard_map/all_to_all | solution.py:346
  312.0 2.3 fusion.1
  314.4 1.4 convolution_add_fusion
  315.8 1.1 copy-done.4
  316.9 0.3 slice.10
  317.1 0.3 copy.81
  317.4 4.0 %collective-permute-start.3 = (bf16[64,2880]{1,0:T(8,128)(2,1)S(1)}, bf16[64,2880]{1,0:T(8,128)(2,1)S(1)}, u32[]{:S(2)}, u32[]{:S(2)}) collective-permute-start(bf16[64,2880]{1,0:T(8,128)(2,1)S(1)} %copy.81), channel_id=1, source_target_pairs={{0,8},{8,0},{1,9},{9,1},{2,10},{10,2},{3,11},{11,3},{4,12},{12,4},... | collective-permute-start | bytes 1105928 | tf_op jit(solution)/shard_map/ppermute | solution.py:193
  321.4 1.8 copy.80
  323.3 0.1 add_convert_fusion
  323.4 0.9 copy.91
  (58 shorter events, 1.3 us)
Async XLA Ops:
  6.5 68.2 %all-gather.5.cloned.1.call-start = ((), (), s32[]{:S(2)}) async-start(), calls=%async_computation.4 | async-start | bytes 11141120 | tf_op jit(solution)/shard_map/all_gather | solution.py:324
  9.0 76.6 %copy-start.12 = (bf16[128,4,512]{2,1,0:T(4,128)(2,1)S(1)}, bf16[128,4,512]{2,1,0:T(4,128)(2,1)}, u32[]{:S(2)}) copy-start(bf16[128,4,512]{2,1,0:T(4,128)(2,1)} %param.11) | copy-start | bytes 1572868
  9.0 76.7 %copy-start.16 = (s32[4]{0:T(128)S(1)}, s32[4]{0:T(128)}, u32[]{:S(2)}) copy-start(s32[4]{0:T(128)} %param.14) | copy-start | bytes 52
  9.0 113.0 %all-gather.7.cloned.1.call-start = ((), (), s32[]{:S(2)}) async-start(), calls=%async_computation.5 | async-start | bytes 3203072 | tf_op jit(solution)/shard_map/all_gather | solution.py:326
  104.0 0.7 copy-start.2
  124.8 1.0 copy-start.3
  125.7 8.8 %copy-start.13 = (s32[16,4,4]{0,2,1:T(4,128)S(1)}, s32[16,4,4]{0,2,1:T(4,128)}, u32[]{:S(2)}) copy-start(s32[16,4,4]{0,2,1:T(4,128)} %param.18) | copy-start | bytes 3076
  125.7 9.4 %copy-start.15 = (f32[16,4,4]{0,2,1:T(4,128)S(1)}, f32[16,4,4]{0,2,1:T(4,128)}, u32[]{:S(2)}) copy-start(f32[16,4,4]{0,2,1:T(4,128)} %param.19) | copy-start | bytes 3076
  126.8 1.2 copy-start.1
  128.0 39.2 %all-to-all-start = ((bf16[8,32,2880]{2,1,0:T(8,128)(2,1)}), bf16[8,32,2880]{2,1,0:T(8,128)(2,1)}, u32[]{:S(2)}, u32[]{:S(2)}) async-start(bf16[8,32,2880]{2,1,0:T(8,128)(2,1)} %copy-done.1), calls=%async_computation | async-start | bytes 3014656 | tf_op jit(solution)/shard_map/all_to_all | solution.py:332
  134.6 39.7 %collective-permute-start = (s32[64,4]{0,1:T(4,128)S(1)}, s32[64,4]{0,1:T(4,128)S(1)}, u32[]{:S(2)}, u32[]{:S(2)}) collective-permute-start(s32[64,4]{0,1:T(4,128)S(1)} %reshape_reshape.3), channel_id=1, source_target_pairs={{0,8},{8,0},{1,9},{9,1},{2,10},{10,2},{3,11},{11,3},{4,12},{12,4},... | collective-permute-start | bytes 3080 | tf_op jit(solution)/shard_map/ppermute | solution.py:193
  135.3 64.2 %collective-permute-start.2 = (f32[64,4]{0,1:T(4,128)S(1)}, f32[64,4]{0,1:T(4,128)S(1)}, u32[]{:S(2)}, u32[]{:S(2)}) collective-permute-start(f32[64,4]{0,1:T(4,128)S(1)} %reshape.53), channel_id=1, source_target_pairs={{0,8},{8,0},{1,9},{9,1},{2,10},{10,2},{3,11},{11,3},{4,12},{12,4},... | collective-permute-start | bytes 3080 | tf_op jit(solution)/shard_map/ppermute | solution.py:193
  165.0 9.2 %copy-start.10 = (bf16[16,4,2880]{2,1,0:T(4,128)(2,1)S(1)}, bf16[16,4,2880]{2,1,0:T(4,128)(2,1)}, u32[]{:S(2)}) copy-start(bf16[16,4,2880]{2,1,0:T(4,128)(2,1)} %param.15) | copy-start | bytes 1105924
  166.1 1.1 copy-start
  167.2 29.2 %all-to-all-start.1 = ((bf16[8,32,2880]{2,1,0:T(8,128)(2,1)}), bf16[8,32,2880]{2,1,0:T(8,128)(2,1)S(1)}, u32[]{:S(2)}, u32[]{:S(2)}) async-start(bf16[8,32,2880]{2,1,0:T(8,128)(2,1)} %copy-done), calls=%async_computation.1 | async-start | bytes 3014656 | tf_op jit(solution)/shard_map/all_to_all | solution.py:332
  174.3 23.0 %copy-start.5 = (f32[4,16,2880]{2,1,0:T(8,128)}, f32[4,16,2880]{2,1,0:T(8,128)S(1)}, u32[]{:S(2)}) copy-start(f32[4,16,2880]{2,1,0:T(8,128)S(1)} %copy.65) | copy-start | bytes 2211844
  174.3 22.4 %copy-start.11 = (bf16[16,4,2880]{2,1,0:T(4,128)(2,1)S(1)}, bf16[16,4,2880]{2,1,0:T(4,128)(2,1)}, u32[]{:S(2)}) copy-start(bf16[16,4,2880]{2,1,0:T(4,128)(2,1)} %param.15) | copy-start | bytes 1105924
  175.0 22.3 %copy-start.14 = (f32[2880]{0:T(1024)S(1)}, f32[2880]{0:T(1024)}, u32[]{:S(2)}) copy-start(f32[2880]{0:T(1024)} %param.17) | copy-start | bytes 34564
  196.6 3.1 copy-start.7
  197.4 2.2 collective-permute-start.1
  268.9 43.2 %all-to-all-start.3 = ((bf16[64,8,2880]{2,1,0:T(8,128)(2,1)}), bf16[64,8,2880]{2,1,0:T(8,128)(2,1)S(1)}, u32[]{:S(2)}, u32[]{:S(2)}) async-start(bf16[64,8,2880]{2,1,0:T(8,128)(2,1)} %bitcast.16), calls=%async_computation.3 | async-start | bytes 6029312 | tf_op jit(solution)/shard_map/all_to_all | solution.py:346
  312.0 2.3 copy-start.9
  315.8 1.1 copy-start.4
  316.9 6.4 %copy-start.6 = (f32[4,16,2880]{2,1,0:T(8,128)S(1)}, f32[4,16,2880]{2,1,0:T(8,128)}, u32[]{:S(2)}) copy-start(f32[4,16,2880]{2,1,0:T(8,128)} %copy-done.5) | copy-start | bytes 2211844
  316.9 6.4 %copy-start.8 = (f32[32,2880]{1,0:T(8,128)S(1)}, f32[32,2880]{1,0:T(8,128)}, u32[]{:S(2)}) copy-start(f32[32,2880]{1,0:T(8,128)} %copy-done.7) | copy-start | bytes 1105924
  317.4 5.8 %collective-permute-start.3 = (bf16[64,2880]{1,0:T(8,128)(2,1)S(1)}, bf16[64,2880]{1,0:T(8,128)(2,1)S(1)}, u32[]{:S(2)}, u32[]{:S(2)}) collective-permute-start(bf16[64,2880]{1,0:T(8,128)(2,1)S(1)} %copy.81), channel_id=1, source_target_pairs={{0,8},{8,0},{1,9},{9,1},{2,10},{10,2},{3,11},{11,3},{4,12},{12,4},... | collective-permute-start | bytes 1105928 | tf_op jit(solution)/shard_map/ppermute | solution.py:193
Sparse Core Ops, SparseCore 0:
  9.1 65.6 all-gather.4
  85.7 36.2 all-gather.6
